TPU v7x, 512 devices: a whole 4x4x16 slice. The times are simulated.
512 devices in a mesh: dp: 16 (over z), expert: 32 (over y, x, core).
Axes of the slice: x: 4, y: 4, z: 16, core: 2. Of those that a mesh axis runs over, the one named last changes fastest.
Arguments:
- tokens: bfloat16 [65536, 1024], P(('dp', 'expert')), may hold values from -6 to 6
- grad_out: bfloat16 [65536, 1024], P(('dp', 'expert')), may hold values from -6 to 6
- expert_ids: int32 [65536, 2], P(('dp', 'expert')), may hold values from 0 to 31, all different within a row; in each aligned block of 128 rows (0 to 127, 128 to 255, ...) at most 16 rows name the same one
- route_probs: bfloat16 [65536, 2], P(('dp', 'expert')), may hold values from 0.19921875 to 1
- gate_up_weight: bfloat16 [1024, 32, 1536], P('dp', 'expert'), may hold values from -0.1875 to 0.1875
- down_weight: bfloat16 [32, 768, 1024], P('expert'), may hold values from -0.21875 to 0.21875
- gate_up_scale_index: int32 [8, 32, 2], P(None, 'expert'), may hold values from 0 to 15
- down_scale_index: int32 [32, 6], P('expert'), may hold values from 0 to 15
- scale_table: float32 [16], replicated, may hold values from 0.5 to 2
Outputs:
- token_grad: bfloat16 [65536, 1024], P(('dp', 'expert'))
- prob_grad: float32 [65536, 2], P(('dp', 'expert'))
- gate_up_grad: bfloat16 [1024, 32, 1536], P('dp', 'expert')
- down_grad: bfloat16 [32, 768, 1024], P('expert')
Inputs may be any that keep to these rules, and one draw needn't show every extreme that they name: `expert_ids`: each row names two different experts. The 128 rows of one device name one expert at most 16 times, and in every draw some device's rows name some expert exactly 16 times.
All inputs are finite; a program needn't handle non-finite values.
Results may differ from a plain program's by a relative error of at most 0.022.
Values may be sent and summed in bfloat16 or wider, within the bound.
No kernel may reach another device: no remote copies, remote signals or barrier semaphores. Data moves between devices by JAX's collectives and lax.ppermute only.
A program may use at most 64 MiB of HBM per device.

v0:
```python
import jax
import jax.numpy as jnp
from jax import lax
from jax.sharding import PartitionSpec as P

QBLOCK = 128


def lookup(level_index, level_table):
    onehot = (level_index[..., None] == jnp.arange(level_table.shape[0], dtype=jnp.int32)).astype(
        level_table.dtype
    )
    return jnp.sum(onehot * level_table, axis=-1)


def slot_tables(routes, experts, capacity):
    flat_routes = routes.reshape(-1)
    expert_hits = (flat_routes[:, None] == jnp.arange(experts, dtype=jnp.int32)[None, :]).astype(
        jnp.int32
    )
    before = jnp.cumsum(expert_hits, axis=0) - expert_hits
    slot_rank = jnp.sum(before * expert_hits, axis=1)
    destination = flat_routes * capacity + slot_rank
    table_hits = destination[:, None] == jnp.arange(experts * capacity, dtype=jnp.int32)[None, :]
    return table_hits.astype(jnp.float32).reshape(routes.shape[0], 2, experts * capacity)


def body(
    tokens,
    grad_out,
    expert_ids,
    route_probs,
    gate_up_weight,
    down_weight,
    gate_up_scale_index,
    down_scale_index,
    scale_table,
):
    high = lax.Precision.HIGHEST
    f32 = jnp.float32
    groups = lax.axis_size("expert")
    tok_dev = tokens.shape[0]
    model_width = tokens.shape[1]
    per_device = down_weight.shape[0]
    hidden = down_weight.shape[1]
    experts = per_device * groups
    capacity = 4 * tok_dev // experts
    slots_all = experts * capacity
    slot_hits = slot_tables(expert_ids, experts, capacity)
    either = (slot_hits[:, 0] + slot_hits[:, 1]).astype(jnp.bfloat16)
    row_shape = (groups, per_device, capacity, model_width)
    send_tokens = (
        jnp.einsum("ts,td->sd", either, tokens, preferred_element_type=f32)
        .astype(jnp.bfloat16)
        .reshape(row_shape)
    )
    send_grads = (
        jnp.einsum("ts,td->sd", either, grad_out, preferred_element_type=f32)
        .astype(jnp.bfloat16)
        .reshape(row_shape)
    )
    send_probs = (
        jnp.einsum("tks,tk->s", slot_hits, route_probs.astype(f32), precision=high)
        .astype(jnp.bfloat16)
        .reshape(row_shape[:3])
    )
    recv_tokens, recv_grads, recv_probs = (
        lax.all_to_all(send_tokens, "expert", split_axis=0, concat_axis=0, tiled=True),
        lax.all_to_all(send_grads, "expert", split_axis=0, concat_axis=0, tiled=True),
        lax.all_to_all(send_probs, "expert", split_axis=0, concat_axis=0, tiled=True),
    )
    level_rows = jnp.repeat(lookup(gate_up_scale_index, scale_table), QBLOCK, axis=0)
    full_scale = jnp.repeat(level_rows, hidden, axis=2)
    down_scale = jnp.repeat(lookup(down_scale_index, scale_table), QBLOCK, axis=1)
    down_eff = (down_weight.astype(f32) * down_scale[:, :, None]).astype(jnp.bfloat16)
    gathered = lax.all_gather(gate_up_weight, "dp", axis=0, tiled=True)
    gate_up_eff = (gathered.astype(f32) * full_scale).astype(jnp.bfloat16)
    projected = jnp.einsum("sjcd,djf->sjcf", recv_tokens, gate_up_eff, preferred_element_type=f32)
    gate_part = projected[..., :hidden]
    up_part = projected[..., hidden:]
    sigmoid_gate = jax.nn.sigmoid(gate_part)
    activated = gate_part * sigmoid_gate
    hidden_rows = (activated * up_part).astype(jnp.bfloat16)
    hidden_grad = jnp.einsum("sjcd,jfd->sjcf", recv_grads, down_eff, preferred_element_type=f32)
    probs_wide = recv_probs.astype(f32)[..., None]
    scaled_grad = probs_wide * hidden_grad
    gate_grad = scaled_grad * up_part * sigmoid_gate * (1.0 + gate_part * (1.0 - sigmoid_gate))
    up_grad = scaled_grad * activated
    joint_grad = jnp.concatenate([gate_grad, up_grad], axis=-1).astype(jnp.bfloat16)
    row_grads = jnp.einsum(
        "sjcf,djf->sjcd", joint_grad, gate_up_eff, preferred_element_type=f32
    ).astype(jnp.bfloat16)
    back_rows = lax.all_to_all(row_grads, "expert", split_axis=0, concat_axis=0, tiled=True)
    token_grad = jnp.dot(
        either, back_rows.reshape(slots_all, model_width), preferred_element_type=f32
    ).astype(jnp.bfloat16)
    expert_out = jnp.einsum("sjcf,jfd->sjcd", hidden_rows, down_eff, preferred_element_type=f32)
    back_out = lax.all_to_all(
        expert_out.astype(jnp.bfloat16), "expert", split_axis=0, concat_axis=0, tiled=True
    ).astype(expert_out.dtype)
    picked = jnp.einsum(
        "tks,sd->tkd", slot_hits, back_out.reshape(slots_all, model_width), precision=high
    )
    prob_grad = jnp.sum(picked * grad_out.astype(f32)[:, None, :], axis=-1)
    weighted = (probs_wide * hidden_rows.astype(f32)).astype(jnp.bfloat16)
    partial_sum = jnp.einsum("sjcd,sjcf->djf", recv_tokens, joint_grad, preferred_element_type=f32)
    gate_up_grad = lax.psum_scatter(
        (partial_sum * full_scale).astype(jnp.bfloat16), "dp", scatter_dimension=0, tiled=True
    )
    down_part = (
        jnp.einsum("sjcf,sjcd->jfd", weighted, recv_grads, preferred_element_type=f32)
        * down_scale[:, :, None]
    )
    down_grad = lax.psum(down_part.astype(jnp.bfloat16), "dp")
    return (token_grad, prob_grad, gate_up_grad, down_grad)


def solution(mesh):
    in_specs = (
        P(("dp", "expert"), None),
        P(("dp", "expert"), None),
        P(("dp", "expert"), None),
        P(("dp", "expert"), None),
        P("dp", "expert", None),
        P("expert", None, None),
        P(None, "expert", None),
        P("expert", None),
        P(),
    )
    out_specs = (
        P(("dp", "expert"), None),
        P(("dp", "expert"), None),
        P("dp", "expert", None),
        P("expert", None, None),
    )
    return jax.shard_map(body, mesh=mesh, in_specs=in_specs, out_specs=out_specs, check_vma=False)
```

profile of v0, /device:TPU:2, one launch (start us, length us, event | category | flops | bytes accessed | tf_op | source)
XLA Modules:
  0.0 354.2 jit_solution(2820792020950934844)
XLA Ops:
  7.2 0.0 copy-start
  7.2 0.0 all-gather.2.cloned.1.call-start
  7.2 0.7 all-gather.2.cloned.1.call-update
  7.9 0.8 copy.80
  8.7 0.1 eq.109
  8.8 0.1 eq.105
  9.0 0.6 reduce-window.6
  9.6 0.2 slice_reduce_fusion
  9.8 0.1 fusion.42
  9.9 0.1 reduce_sum.39
  10.1 0.1 copy.83
  10.1 0.7 multiply_add_fusion
  10.8 0.9 fusion.32
  11.8 0.7 reshape.263
  12.5 9.4 %all-to-all-start = ((bf16[32,1,16]{2,1,0:T(2,128)(2,1)}), bf16[32,1,16]{2,1,0:T(2,128)(2,1)S(1)}, u32[]{:S(2)}, u32[]{:S(2)}) async-start(bf16[32,1,16]{2,1,0:T(2,128)(2,1)} %reshape.263), calls=%async_computation | async-start | bytes 32768 | tf_op jit(solution)/shard_map/all_to_all | solution.py:70
  21.9 0.1 fusion.33
  22.0 0.0 copy-start.9
  22.0 0.0 copy-start.4
  22.1 1.4 convolution_convert_fusion.1
  23.5 4.5 %all-to-all-done = bf16[32,1,16]{2,1,0:T(2,128)(2,1)S(1)} async-done(((bf16[32,1,16]{2,1,0:T(2,128)(2,1)}), bf16[32,1,16]{2,1,0:T(2,128)(2,1)S(1)}, u32[]{:S(2)}, u32[]{:S(2)}) %all-to-all-start) | async-done | bytes 1056 | tf_op jit(solution)/shard_map/all_to_all | solution.py:70
  28.0 5.7 %all-to-all-start.2 = ((bf16[32,1,16,1024]{3,2,1,0:T(8,128)(2,1)}), bf16[32,1,16,1024]{3,2,1,0:T(8,128)(2,1)}, u32[]{:S(2)}, u32[]{:S(2)}) async-start(bf16[32,1,16,1024]{3,2,1,0:T(8,128)(2,1)} %bitcast.20), calls=%async_computation.2 | async-start | bytes 2097152 | tf_op jit(solution)/shard_map/all_to_all | solution.py:68
  33.8 0.2 select_reduce_fusion
  33.9 0.1 broadcast_bitcast_fusion
  34.0 0.2 fusion.44
  34.2 0.7 broadcast_bitcast_fusion.1
  34.9 1.4 convolution_convert_fusion.2
  36.3 0.1 copy.86
  36.4 54.6 %all-gather.2.cloned.1.call-done = bf16[1024,1,1536]{2,0,1:T(8,128)(2,1)} async-done(((bf16[64,1,1536]{2,0,1:T(8,128)(2,1)}), bf16[1024,1,1536]{2,0,1:T(8,128)(2,1)}) %all-gather.2.cloned.1.call-update) | async-done | bytes 3145744 | tf_op jit(solution)/shard_map/all_gather | solution.py:76
  91.0 3.2 copy.84
  94.2 7.4 %all-to-all-start.1 = ((bf16[32,1,16,1024]{3,2,1,0:T(8,128)(2,1)}), bf16[32,1,16,1024]{3,2,1,0:T(8,128)(2,1)}, u32[]{:S(2)}, u32[]{:S(2)}) async-start(bf16[32,1,16,1024]{3,2,1,0:T(8,128)(2,1)} %bitcast.158), calls=%async_computation.1 | async-start | bytes 2097152 | tf_op jit(solution)/shard_map/all_to_all | solution.py:69
  101.7 0.2 reduce-scatter.4.cloned.1.call-start
  101.9 0.8 broadcast_in_dim.28
  102.7 1.2 fusion.3
  103.9 1.7 copy-done.1
  105.5 1.7 copy-done.2
  107.3 5.1 %convolution_bitcast_fusion = f32[32,1,16,1536]{3,0,2,1:T(8,128)} fusion(bf16[1024,1536,1]{0,1,2:T(8,128)(2,1)S(1)} %fusion.3, bf16[32,1,16,1024]{3,2,1,0:T(8,128)(2,1)} %all-to-all-done.2), kind=kOutput, calls=%fused_computation.4 | convolution fusion | flops 1610612736 | bytes 7340032 | tf_op jit(solution)/shard_map/sjcd,djf->sjcf/dot_general | solution.py:78
  112.3 5.5 %all-to-all-done.1 = bf16[32,1,16,1024]{3,2,1,0:T(8,128)(2,1)} async-done(((bf16[32,1,16,1024]{3,2,1,0:T(8,128)(2,1)}), bf16[32,1,16,1024]{3,2,1,0:T(8,128)(2,1)}, u32[]{:S(2)}, u32[]{:S(2)}) %all-to-all-start.1) | async-done | bytes 1048608 | tf_op jit(solution)/shard_map/all_to_all | solution.py:69
  117.8 5.3 %fusion.29 = (bf16[32,16,768]{2,0,1:T(8,128)(2,1)S(1)}, bf16[32,16,768]{2,0,1:T(8,128)(2,1)S(1)}, bf16[32,1,16,768]{3,0,2,1:T(8,128)(2,1)}) fusion(f32[32,1,16,1536]{3,0,2,1:T(8,128)} %convolution_bitcast_fusion, bf16[32,1,16,1024]{3,2,1,0:T(8,128)(2,1)} %all-to-all-done.1, bf16[1,768,1024]{2,1,0:T(8,128)(2,1)S(1)} %copy-done.11, f32[768]{0:T(1024)S(1)} %copy-done.8, ...), kind=kOutput, calls=%fused_computation.46 | convolution fusion | flops 813957120 | bytes 8131584 | tf_op jit(solution)/shard_map/sjcd,jfd->sjcf/dot_general | solution.py:84
  123.2 3.8 %fusion.15 = f32[1536,1024,1]{1,0,2:T(8,128)S(1)} fusion(bf16[32,16,768]{2,0,1:T(8,128)(2,1)S(1)} %get-tuple-element.25, bf16[32,16,768]{2,0,1:T(8,128)(2,1)S(1)} %get-tuple-element.24, bf16[32,1,16,1024]{3,2,1,0:T(8,128)(2,1)} %all-to-all-done.2), kind=kOutput, calls=%fused_computation.33 | convolution fusion | flops 1613758464 | bytes 8912896 | tf_op jit(solution)/shard_map/sjcd,sjcf->djf/dot_general | solution.py:106
  127.0 1.8 fusion.2
  128.8 3.0 copy.104
  131.8 0.0 reduce-scatter.4.cloned.1.call-update
  131.8 1.4 copy-done.12
  133.2 0.2 copy-done.14
  133.4 1.1 fusion.12
  134.5 1.5 copy.94
  136.0 5.7 %all-to-all-start.4 = ((bf16[32,1,16,1024]{3,2,1,0:T(8,128)(2,1)}), bf16[32,1,16,1024]{3,2,1,0:T(8,128)(2,1)}, u32[]{:S(2)}, u32[]{:S(2)}) async-start(bf16[32,1,16,1024]{3,2,1,0:T(8,128)(2,1)} %copy.94), calls=%async_computation.4 | async-start | bytes 2097152 | tf_op jit(solution)/shard_map/all_to_all | solution.py:98
  141.8 0.3 all-reduce.2.cloned.1.call-start
  142.0 4.1 %fusion.11 = bf16[1,768,1024]{2,1,0:T(8,128)(2,1)} fusion(f32[768]{0:T(1024)S(1)} %copy-done.8, bf16[32,1,16,1024]{3,2,1,0:T(8,128)(2,1)} %all-to-all-done.1, bf16[32,1,16,768]{3,0,2,1:T(8,128)(2,1)} %get-tuple-element.26, f32[32,16]{0,1:T(8,128)S(1)} %copy.86), kind=kOutput, calls=%fused_computation.23 | convolution fusion | flops 808058880 | bytes 3412992 | tf_op jit(solution)/shard_map/sjcf,sjcd->jfd/dot_general | solution.py:111
  146.1 0.0 all-reduce.2.cloned.1.call-update
  146.2 3.2 fusion.13
  149.3 0.0 copy-start.5
  149.3 0.0 copy-start.7
  149.3 1.6 copy.93
  150.9 7.1 %all-to-all-done.4 = bf16[32,1,16,1024]{3,2,1,0:T(8,128)(2,1)} async-done(((bf16[32,1,16,1024]{3,2,1,0:T(8,128)(2,1)}), bf16[32,1,16,1024]{3,2,1,0:T(8,128)(2,1)}, u32[]{:S(2)}, u32[]{:S(2)}) %all-to-all-start.4) | async-done | bytes 1048608 | tf_op jit(solution)/shard_map/all_to_all | solution.py:98
  158.0 5.0 %all-to-all-start.3 = ((bf16[32,1,16,1024]{3,2,1,0:T(8,128)(2,1)}), bf16[32,1,16,1024]{3,2,1,0:T(8,128)(2,1)S(1)}, u32[]{:S(2)}, u32[]{:S(2)}) async-start(bf16[32,1,16,1024]{3,2,1,0:T(8,128)(2,1)} %copy.93), calls=%async_computation.3 | async-start | bytes 2097152 | tf_op jit(solution)/shard_map/all_to_all | solution.py:93
  163.1 2.4 fusion.14
  165.5 13.8 %all-to-all-done.3 = bf16[32,1,16,1024]{3,2,1,0:T(8,128)(2,1)S(1)} async-done(((bf16[32,1,16,1024]{3,2,1,0:T(8,128)(2,1)}), bf16[32,1,16,1024]{3,2,1,0:T(8,128)(2,1)S(1)}, u32[]{:S(2)}, u32[]{:S(2)}) %all-to-all-start.3) | async-done | bytes 1048608 | tf_op jit(solution)/shard_map/all_to_all | solution.py:93
  179.3 1.0 convolution_convert_fusion.4
  180.3 22.1 %reduce-scatter.4.cloned.1.call-done = bf16[64,1536]{1,0:T(8,128)(2,1)} async-done(((bf16[1024,1536]{1,0:T(8,128)(2,1)}), bf16[64,1536]{1,0:T(8,128)(2,1)}) %reduce-scatter.4.cloned.1.call-update) | async-done | bytes 196624
  202.4 1.1 copy.105
  203.6 0.8 copy.96
  204.4 140.6 %all-reduce.2.cloned.1.call-done = bf16[1,768,1024]{2,1,0:T(8,128)(2,1)} async-done(((bf16[1,768,1024]{2,1,0:T(8,128)(2,1)}), bf16[1,768,1024]{2,1,0:T(8,128)(2,1)}) %all-reduce.2.cloned.1.call-update) | async-done | bytes 1572880 | tf_op jit(solution)/shard_map/psum | solution.py:114
  345.0 2.7 copy.132
  (39 shorter events, 0.2 us)
Async XLA Ops:
  7.2 14.9 %copy-start = (bf16[128,1024]{1,0:T(8,128)(2,1)S(1)}, bf16[128,1024]{1,0:T(8,128)(2,1)}, u32[]{:S(2)}) copy-start(bf16[128,1024]{1,0:T(8,128)(2,1)} %param.9) | copy-start | bytes 786436
  7.2 83.8 %all-gather.2.cloned.1.call-start = ((), (), s32[]{:S(2)}) async-start(), calls=%async_computation.6 | async-start | bytes 3342336 | tf_op jit(solution)/shard_map/all_gather | solution.py:76
  10.8 11.0 %copy-start.6 = (s32[128,2]{0,1:T(2,128)}, s32[128,2]{0,1:T(2,128)S(1)}, u32[]{:S(2)}) copy-start(s32[128,2]{0,1:T(2,128)S(1)} %multiply_add_fusion) | copy-start | bytes 3076
  12.5 15.6 %all-to-all-start = ((bf16[32,1,16]{2,1,0:T(2,128)(2,1)}), bf16[32,1,16]{2,1,0:T(2,128)(2,1)S(1)}, u32[]{:S(2)}, u32[]{:S(2)}) async-start(bf16[32,1,16]{2,1,0:T(2,128)(2,1)} %reshape.263), calls=%async_computation | async-start | bytes 32768 | tf_op jit(solution)/shard_map/all_to_all | solution.py:70
  22.0 11.8 %copy-start.9 = (s32[8,1,2]{0,2,1:T(2,128)S(1)}, s32[8,1,2]{0,2,1:T(2,128)}, u32[]{:S(2)}) copy-start(s32[8,1,2]{0,2,1:T(2,128)} %param.15) | copy-start | bytes 196
  22.0 11.8 %copy-start.10 = (f32[16]{0:T(128)S(1)}, f32[16]{0:T(128)}, u32[]{:S(2)}) copy-start(f32[16]{0:T(128)} %param.17) | copy-start | bytes 196
  22.0 12.0 %copy-start.13 = (s32[1,6]{1,0:T(1,128)S(1)}, s32[1,6]{1,0:T(1,128)}, u32[]{:S(2)}) copy-start(s32[1,6]{1,0:T(1,128)} %param.16) | copy-start | bytes 76
  22.0 12.9 %copy-start.4 = (bf16[128,1024]{1,0:T(8,128)(2,1)S(1)}, bf16[128,1024]{1,0:T(8,128)(2,1)}, u32[]{:S(2)}) copy-start(bf16[128,1024]{1,0:T(8,128)(2,1)} %param.10) | copy-start | bytes 786436
  28.0 66.2 %all-to-all-start.2 = ((bf16[32,1,16,1024]{3,2,1,0:T(8,128)(2,1)}), bf16[32,1,16,1024]{3,2,1,0:T(8,128)(2,1)}, u32[]{:S(2)}, u32[]{:S(2)}) async-start(bf16[32,1,16,1024]{3,2,1,0:T(8,128)(2,1)} %bitcast.20), calls=%async_computation.2 | async-start | bytes 2097152 | tf_op jit(solution)/shard_map/all_to_all | solution.py:68
  94.2 23.6 %all-to-all-start.1 = ((bf16[32,1,16,1024]{3,2,1,0:T(8,128)(2,1)}), bf16[32,1,16,1024]{3,2,1,0:T(8,128)(2,1)}, u32[]{:S(2)}, u32[]{:S(2)}) async-start(bf16[32,1,16,1024]{3,2,1,0:T(8,128)(2,1)} %bitcast.158), calls=%async_computation.1 | async-start | bytes 2097152 | tf_op jit(solution)/shard_map/all_to_all | solution.py:69
  101.7 100.8 %reduce-scatter.4.cloned.1.call-start = ((), (), s32[]{:S(2)}) async-start(), calls=%async_computation.8 | async-start | bytes 3342336
  102.7 2.9 copy-start.1
  105.5 1.7 copy-start.2
  107.3 10.6 %copy-start.8 = (f32[768]{0:T(1024)S(1)}, f32[768]{0:T(1024)}, u32[]{:S(2)}) copy-start(f32[768]{0:T(1024)} %broadcast_bitcast_fusion.1) | copy-start | bytes 9220
  107.3 10.6 %copy-start.11 = (bf16[1,768,1024]{2,1,0:T(8,128)(2,1)S(1)}, bf16[1,768,1024]{2,1,0:T(8,128)(2,1)}, u32[]{:S(2)}) copy-start(bf16[1,768,1024]{2,1,0:T(8,128)(2,1)} %param.14) | copy-start | bytes 4718596
  117.8 9.2 %slice-start = ((s8[6291456]{0:T(1024)(128)(4,1)}), s8[4194304]{0:T(1024)(128)(4,1)S(1)}, s32[]{:S(2)}) async-start(s8[6291456]{0:T(1024)(128)(4,1)} %bitcast.155), calls=%async_computation.9 | async-start | bytes 8388608
  123.1 3.8 %copy-start.15 = (bf16[32,16,768]{2,0,1:T(8,128)(2,1)}, bf16[32,16,768]{2,0,1:T(8,128)(2,1)S(1)}, u32[]{:S(2)}) copy-start(bf16[32,16,768]{2,0,1:T(8,128)(2,1)S(1)} %get-tuple-element.24) | copy-start | bytes 2359300
  123.1 3.8 %copy-start.16 = (bf16[32,16,768]{2,0,1:T(8,128)(2,1)}, bf16[32,16,768]{2,0,1:T(8,128)(2,1)S(1)}, u32[]{:S(2)}) copy-start(bf16[32,16,768]{2,0,1:T(8,128)(2,1)S(1)} %get-tuple-element.25) | copy-start | bytes 2359300
  123.1 3.9 %slice-start.1 = ((s8[6291456]{0:T(1024)(128)(4,1)}), s8[2097152]{0:T(1024)(128)(4,1)S(1)}, s32[]{:S(2)}) async-start(s8[6291456]{0:T(1024)(128)(4,1)} %bitcast.155), calls=%async_computation.10 | async-start | bytes 4194304
  131.8 1.4 copy-start.12
  131.8 1.6 copy-start.14
  136.0 22.0 %all-to-all-start.4 = ((bf16[32,1,16,1024]{3,2,1,0:T(8,128)(2,1)}), bf16[32,1,16,1024]{3,2,1,0:T(8,128)(2,1)}, u32[]{:S(2)}, u32[]{:S(2)}) async-start(bf16[32,1,16,1024]{3,2,1,0:T(8,128)(2,1)} %copy.94), calls=%async_computation.4 | async-start | bytes 2097152 | tf_op jit(solution)/shard_map/all_to_all | solution.py:98
  141.8 4.4 %copy-start.3 = (bf16[1024,1536,1]{0,1,2:T(8,128)(2,1)S(1)}, bf16[1024,1536,1]{0,1,2:T(8,128)(2,1)}, u32[]{:S(2)}) copy-start(bf16[1024,1536,1]{0,1,2:T(8,128)(2,1)} %copy-done.2) | copy-start | bytes 9437188
  141.8 203.2 %all-reduce.2.cloned.1.call-start = ((), (), s32[]{:S(2)}) async-start(), calls=%async_computation.7 | async-start | bytes 3145728 | tf_op jit(solution)/shard_map/psum | solution.py:114
  149.3 13.7 %copy-start.5 = (bf16[128,1024]{1,0:T(8,128)(2,1)S(1)}, bf16[128,1024]{1,0:T(8,128)(2,1)}, u32[]{:S(2)}) copy-start(bf16[128,1024]{1,0:T(8,128)(2,1)} %param.10) | copy-start | bytes 786436
  149.3 13.8 %copy-start.7 = (s32[128,2]{0,1:T(2,128)S(1)}, s32[128,2]{0,1:T(2,128)}, u32[]{:S(2)}) copy-start(s32[128,2]{0,1:T(2,128)} %copy-done.6) | copy-start | bytes 3076
  158.0 21.3 %all-to-all-start.3 = ((bf16[32,1,16,1024]{3,2,1,0:T(8,128)(2,1)}), bf16[32,1,16,1024]{3,2,1,0:T(8,128)(2,1)S(1)}, u32[]{:S(2)}, u32[]{:S(2)}) async-start(bf16[32,1,16,1024]{3,2,1,0:T(8,128)(2,1)} %copy.93), calls=%async_computation.3 | async-start | bytes 2097152 | tf_op jit(solution)/shard_map/all_to_all | solution.py:93
Sparse Core Ops, SparseCore 0:
  10.1 80.8 all-gather.1
  131.9 70.4 reduce-scatter.3
  205.3 139.6 all-reduce.1
where the time goes:
time: 355 us; the launch traced here: 354 us
  waiting for transfers between devices  249 us (70%)
  starting transfers between devices  33.8 us (10%)
  matrix products  29.7 us (8%)
  local copies, waits for them, and re-layouts  22.7 us (6%)
  between operations  14.1 us (4%)
  other arithmetic  4.95 us (1%)
    psum x1, waiting for transfers between devices, body(): down_grad = lax.psum(down_part.astype(jnp.bfloat16), 'dp')  141 us
    all_gather x1, waiting for transfers between devices, body(): gathered = lax.all_gather(gate_up_weight, 'dp', axis=0, tiled=True)  54.6 us
    unnamed x4, waiting for transfers between devices  22.8 us
    all_to_all x1, waiting for transfers between devices, body(): lax.all_to_all(row_grads, 'expert', split_axis=0, concat_axis=0, tiled=True)  13.8 us
    unnamed x45, local copies, waits for them, and re-layouts  13.5 us
    all_to_all x1, starting transfers between devices, body(): lax.all_to_all(send_probs, 'expert', split_axis=0, concat_axis=0, tiled=T...  9.4 us
    all_to_all x1, starting transfers between devices, body(): lax.all_to_all(send_grads, 'expert', split_axis=0, concat_axis=0, tiled=T...  7.43 us
  transfers between devices with their start and end apart: 8, of which 7 were waited for; matrix products, arithmetic and copies ran while one was open for 10% of the time, Pallas kernels for 0%

commit v1 on v0

--- a/solution.py
+++ b/solution.py
@@ -1,9 +1,31 @@
+import functools
 import jax
 import jax.numpy as jnp
 from jax import lax
 from jax.sharding import PartitionSpec as P
+from jax.lax import axis_index, axis_size, ppermute
 
 QBLOCK = 128
+
+
+def pairs_all_lay(z, across):
+    ndev = axis_size(across)
+    ledger = [(dev_j, (dev_j + 1) % ndev) for dev_j in range(ndev)]
+    n_now, y1 = ([z], [z])
+    in_order = [(dev_j, (dev_j - 1) % ndev) for dev_j in range(ndev)]
+    for _ in range(ndev // 2):
+        n_now.append(ppermute(n_now[-1], axis_name=across, perm=ledger))
+    for _ in range((ndev - 1) // 2):
+        y1.append(ppermute(y1[-1], axis_name=across, perm=in_order))
+    w_next = jnp.roll(
+        jnp.concatenate([*n_now[::-1], *y1[1:]], 0),
+        (axis_index(across) - ndev // 2) * z.shape[0],
+        axis=0,
+    )
+    return w_next
+
+
+seats_all_move = functools.partial(pairs_all_lay, across="dp")
 
 
 def lookup(level_index, level_table):
@@ -73,7 +95,7 @@
     full_scale = jnp.repeat(level_rows, hidden, axis=2)
     down_scale = jnp.repeat(lookup(down_scale_index, scale_table), QBLOCK, axis=1)
     down_eff = (down_weight.astype(f32) * down_scale[:, :, None]).astype(jnp.bfloat16)
-    gathered = lax.all_gather(gate_up_weight, "dp", axis=0, tiled=True)
+    gathered = seats_all_move(gate_up_weight)
     gate_up_eff = (gathered.astype(f32) * full_scale).astype(jnp.bfloat16)
     projected = jnp.einsum("sjcd,djf->sjcf", recv_tokens, gate_up_eff, preferred_element_type=f32)
     gate_part = projected[..., :hidden]

time: 355 us -> 412 us (1.16)
  starting transfers between devices: 33.8 us -> 93.1 us
  waiting for transfers between devices: 249 us -> 219 us
  local copies, waits for them, and re-layouts: 22.7 us -> 42.2 us
    ppermute x0 -> x15, starting transfers between devices: none -> 59.4 us  [the longest x7 42.1 us: pairs_all_lay(): y1.append(ppermute(y1[-1], axis_name=across, perm=in_order))]
    all_gather x1 -> x0, waiting for transfers between devices: 54.6 us -> none  [body(): gathered = lax.all_gather(gate_up_weight, 'dp', axis=0, tiled=True)]
    ppermute x0 -> x15, waiting for transfers between devices: none -> 33.3 us  [the longest x7 23.7 us: pairs_all_lay(): y1.append(ppermute(y1[-1], axis_name=across, perm=in_order))]
    concatenate x0 -> x1, local copies, waits for them, and re-layouts: none -> 16.5 us  [pairs_all_lay(): jnp.roll(jnp.concatenate([*n_now[::-1], *y1[1:]], 0), (axis_index(across)...]
    unnamed x45 -> x42, local copies, waits for them, and re-layouts: 13.5 us -> 19 us
    all_to_all x1, waiting for transfers between devices: 4.52 us -> 0.01 us  [body(): lax.all_to_all(send_probs, 'expert', split_axis=0, concat_axis=0, tiled=T...]
    unnamed x4 -> x3, waiting for transfers between devices: 22.8 us -> 23.2 us
  transfers between devices with their start and end apart: 8 -> 22, of which waited for: 7 -> 12; matrix products, arithmetic and copies ran while one was open for 10% -> 14% of each run, Pallas kernels for 0% -> 0%
where the time goes in v1:
time: 412 us; the launch traced here: 409 us
  waiting for transfers between devices  219 us (53%)
  starting transfers between devices  93.1 us (23%)
  local copies, waits for them, and re-layouts  42.2 us (10%)
  matrix products  31.9 us (8%)
  between operations  14.6 us (4%)
  other arithmetic  7.89 us (2%)
    psum x1, waiting for transfers between devices, body(): down_grad = lax.psum(down_part.astype(jnp.bfloat16), 'dp')  140 us
    ppermute x7, starting transfers between devices, pairs_all_lay(): y1.append(ppermute(y1[-1], axis_name=across, perm=in_order))  42.1 us
    ppermute x7, waiting for transfers between devices, pairs_all_lay(): y1.append(ppermute(y1[-1], axis_name=across, perm=in_order))  23.7 us
    unnamed x3, waiting for transfers between devices  23.2 us
    unnamed x42, local copies, waits for them, and re-layouts  19 us
    ppermute x8, starting transfers between devices, pairs_all_lay(): n_now.append(ppermute(n_now[-1], axis_name=across, perm=ledger))  17.3 us
    concatenate x1, local copies, waits for them, and re-layouts, pairs_all_lay(): jnp.roll(jnp.concatenate([*n_now[::-1], *y1[1:]], 0), (axis_index(across)...  16.5 us
    all_to_all x1, waiting for transfers between devices, body(): lax.all_to_all(row_grads, 'expert', split_axis=0, concat_axis=0, tiled=True)  13.8 us
  transfers between devices with their start and end apart: 22, of which 12 were waited for; matrix products, arithmetic and copies ran while one was open for 14% of the time, Pallas kernels for 0%

profile of v1, /device:TPU:2, one launch (start us, length us, event | category | flops | bytes accessed | tf_op | source)
XLA Modules:
  0.0 409.1 jit_solution(17823563916355118716)
XLA Ops:
  7.2 1.2 copy.96
  8.4 3.8 collective-permute-start
  12.2 9.5 %collective-permute-start.8 = (bf16[64,1,1536]{0,2,1:T(8,128)(2,1)S(1)}, bf16[64,1,1536]{0,2,1:T(8,128)(2,1)S(1)}, u32[]{:S(2)}, u32[]{:S(2)}) collective-permute-start(bf16[64,1,1536]{0,2,1:T(8,128)(2,1)S(1)} %copy.96), channel_id=1, source_target_pairs={{0,480},{32,0},{64,32},{96,64},{128,96},{160,128},{192,160},{224,1... | collective-permute-start | bytes 589832 | tf_op jit(solution)/shard_map/ppermute | solution.py:19
  21.7 0.8 copy.92
  23.9 0.7 multiply_add_fusion
  24.6 4.2 %collective-permute-done = bf16[64,1,1536]{0,2,1:T(8,128)(2,1)S(1)} collective-permute-done((bf16[64,1,1536]{0,2,1:T(8,128)(2,1)S(1)}, bf16[64,1,1536]{0,2,1:T(8,128)(2,1)S(1)}, u32[]{:S(2)}, u32[]{:S(2)}) %collective-permute-start) | collective-permute-done | bytes 196640 | tf_op jit(solution)/shard_map/ppermute | solution.py:17
  28.9 1.9 collective-permute-start.1
  30.8 0.9 fusion.32
  31.7 0.7 reshape.263
  32.4 7.6 %all-to-all-start = ((bf16[32,1,16]{2,1,0:T(2,128)(2,1)}), bf16[32,1,16]{2,1,0:T(2,128)(2,1)S(1)}, u32[]{:S(2)}, u32[]{:S(2)}) async-start(bf16[32,1,16]{2,1,0:T(2,128)(2,1)} %reshape.263), calls=%async_computation | async-start | bytes 32768 | tf_op jit(solution)/shard_map/all_to_all | solution.py:92
  40.1 5.1 %collective-permute-start.9 = (bf16[64,1,1536]{0,2,1:T(8,128)(2,1)S(1)}, bf16[64,1,1536]{0,2,1:T(8,128)(2,1)S(1)}, u32[]{:S(2)}, u32[]{:S(2)}) collective-permute-start(bf16[64,1,1536]{0,2,1:T(8,128)(2,1)S(1)} %collective-permute-done.8), channel_id=1, source_target_pairs={{0,480},{32,0},{64,32},{96,64},{128,96},{160,128},{192,160},{224,1... | collective-permute-start | bytes 589832 | tf_op jit(solution)/shard_map/ppermute | solution.py:19
  45.2 1.9 collective-permute-start.2
  47.3 6.6 %collective-permute-done.9 = bf16[64,1,1536]{0,2,1:T(8,128)(2,1)S(1)} collective-permute-done((bf16[64,1,1536]{0,2,1:T(8,128)(2,1)S(1)}, bf16[64,1,1536]{0,2,1:T(8,128)(2,1)S(1)}, u32[]{:S(2)}, u32[]{:S(2)}) %collective-permute-start.9) | collective-permute-done | bytes 196640 | tf_op jit(solution)/shard_map/ppermute | solution.py:19
  53.9 5.6 %collective-permute-start.10 = (bf16[64,1,1536]{0,2,1:T(8,128)(2,1)S(1)}, bf16[64,1,1536]{0,2,1:T(8,128)(2,1)S(1)}, u32[]{:S(2)}, u32[]{:S(2)}) collective-permute-start(bf16[64,1,1536]{0,2,1:T(8,128)(2,1)S(1)} %collective-permute-done.9), channel_id=1, source_target_pairs={{0,480},{32,0},{64,32},{96,64},{128,96},{160,128},{192,160},{224,1... | collective-permute-start | bytes 589832 | tf_op jit(solution)/shard_map/ppermute | solution.py:19
  59.5 1.9 collective-permute-start.3
  61.5 5.9 %collective-permute-done.10 = bf16[64,1,1536]{0,2,1:T(8,128)(2,1)S(1)} collective-permute-done((bf16[64,1,1536]{0,2,1:T(8,128)(2,1)S(1)}, bf16[64,1,1536]{0,2,1:T(8,128)(2,1)S(1)}, u32[]{:S(2)}, u32[]{:S(2)}) %collective-permute-start.10) | collective-permute-done | bytes 196640 | tf_op jit(solution)/shard_map/ppermute | solution.py:19
  67.3 5.6 %collective-permute-start.11 = (bf16[64,1,1536]{0,2,1:T(8,128)(2,1)S(1)}, bf16[64,1,1536]{0,2,1:T(8,128)(2,1)}, u32[]{:S(2)}, u32[]{:S(2)}) collective-permute-start(bf16[64,1,1536]{0,2,1:T(8,128)(2,1)S(1)} %collective-permute-done.10), channel_id=1, source_target_pairs={{0,480},{32,0},{64,32},{96,64},{128,96},{160,128},{192,160},{224,1... | collective-permute-start | bytes 589832 | tf_op jit(solution)/shard_map/ppermute | solution.py:19
  72.9 1.9 collective-permute-start.4
  74.9 1.4 convolution_convert_fusion.1
  76.3 7.4 %all-to-all-start.2 = ((bf16[32,1,16,1024]{3,2,1,0:T(8,128)(2,1)}), bf16[32,1,16,1024]{3,2,1,0:T(8,128)(2,1)}, u32[]{:S(2)}, u32[]{:S(2)}) async-start(bf16[32,1,16,1024]{3,2,1,0:T(8,128)(2,1)} %bitcast.20), calls=%async_computation.2 | async-start | bytes 2097152 | tf_op jit(solution)/shard_map/all_to_all | solution.py:90
  83.7 0.9 select_reduce_fusion
  84.6 5.1 %collective-permute-start.12 = (bf16[64,1,1536]{0,2,1:T(8,128)(2,1)}, bf16[64,1,1536]{0,2,1:T(8,128)(2,1)}, u32[]{:S(2)}, u32[]{:S(2)}) collective-permute-start(bf16[64,1,1536]{0,2,1:T(8,128)(2,1)} %collective-permute-done.11), channel_id=1, source_target_pairs={{0,480},{32,0},{64,32},{96,64},{128,96},{160,128},{192,160},{224,1... | collective-permute-start | bytes 589832 | tf_op jit(solution)/shard_map/ppermute | solution.py:19
  89.7 1.9 collective-permute-start.5
  92.3 1.3 copy.145
  93.6 0.9 fusion.44
  94.5 4.2 %collective-permute-done.12 = bf16[64,1,1536]{0,2,1:T(8,128)(2,1)} collective-permute-done((bf16[64,1,1536]{0,2,1:T(8,128)(2,1)}, bf16[64,1,1536]{0,2,1:T(8,128)(2,1)}, u32[]{:S(2)}, u32[]{:S(2)}) %collective-permute-start.12) | collective-permute-done | bytes 196640 | tf_op jit(solution)/shard_map/ppermute | solution.py:19
  98.7 5.6 %collective-permute-start.13 = (bf16[64,1,1536]{0,2,1:T(8,128)(2,1)}, bf16[64,1,1536]{0,2,1:T(8,128)(2,1)}, u32[]{:S(2)}, u32[]{:S(2)}) collective-permute-start(bf16[64,1,1536]{0,2,1:T(8,128)(2,1)} %collective-permute-done.12), channel_id=1, source_target_pairs={{0,480},{32,0},{64,32},{96,64},{128,96},{160,128},{192,160},{224,1... | collective-permute-start | bytes 589832 | tf_op jit(solution)/shard_map/ppermute | solution.py:19
  104.3 1.9 collective-permute-start.6
  106.2 2.4 convolution_convert_fusion.2
  108.6 3.8 collective-permute-done.13
  112.4 5.6 %collective-permute-start.14 = (bf16[64,1,1536]{0,2,1:T(8,128)(2,1)}, bf16[64,1,1536]{0,2,1:T(8,128)(2,1)}, u32[]{:S(2)}, u32[]{:S(2)}) collective-permute-start(bf16[64,1,1536]{0,2,1:T(8,128)(2,1)} %collective-permute-done.13), channel_id=1, source_target_pairs={{0,480},{32,0},{64,32},{96,64},{128,96},{160,128},{192,160},{224,1... | collective-permute-start | bytes 589832 | tf_op jit(solution)/shard_map/ppermute | solution.py:19
  118.1 1.9 collective-permute-start.7
  121.3 0.8 copy.101
  122.1 3.2 collective-permute-done.14
  125.3 5.3 %collective-permute-done.7 = bf16[64,1,1536]{0,2,1:T(8,128)(2,1)} collective-permute-done((bf16[64,1,1536]{0,2,1:T(8,128)(2,1)}, bf16[64,1,1536]{0,2,1:T(8,128)(2,1)}, u32[]{:S(2)}, u32[]{:S(2)}) %collective-permute-start.7) | collective-permute-done | bytes 196640 | tf_op jit(solution)/shard_map/ppermute | solution.py:17
  130.6 16.5 %concatenate.18 = bf16[2048,1,1536]{0,2,1:T(8,128)(2,1)} concatenate(bf16[64,1,1536]{0,2,1:T(8,128)(2,1)} %collective-permute-done.7, bf16[64,1,1536]{0,2,1:T(8,128)(2,1)} %collective-permute-done.6, bf16[64,1,1536]{0,2,1:T(8,128)(2,1)} %collective-permute-done.5, bf16[64,1,1536]{0,2,1:T(8,128)(2,1)} %collective-permute-done.4, bf16[64,1,1536]{0,2,1:T(8,128)(2,1)S(1)} %collective-permute-done.3, ...), dimensions={0} | concatenate | bytes 12582912 | tf_op jit(solution)/shard_map/jit(_roll_dynamic)/concatenate | solution.py:20
  147.2 7.4 %all-to-all-start.1 = ((bf16[32,1,16,1024]{3,2,1,0:T(8,128)(2,1)}), bf16[32,1,16,1024]{3,2,1,0:T(8,128)(2,1)S(1)}, u32[]{:S(2)}, u32[]{:S(2)}) async-start(bf16[32,1,16,1024]{3,2,1,0:T(8,128)(2,1)} %bitcast.14), calls=%async_computation.1 | async-start | bytes 2097152 | tf_op jit(solution)/shard_map/all_to_all | solution.py:91
  154.8 0.8 broadcast_in_dim.28
  155.6 4.2 %copy-done.2 = bf16[2048,1,1536]{0,2,1:T(8,128)(2,1)S(1)} copy-done((bf16[2048,1,1536]{0,2,1:T(8,128)(2,1)S(1)}, bf16[2048,1,1536]{0,2,1:T(8,128)(2,1)}, u32[]{:S(2)}) %copy-start.2) | copy-done | bytes 6291480
  159.9 2.2 fusion.3
  162.1 1.7 copy-done.3
  163.8 5.3 %convolution_bitcast_fusion = f32[32,1,16,1536]{3,0,2,1:T(8,128)} fusion(bf16[1024,1536,1]{0,1,2:T(8,128)(2,1)S(1)} %fusion.3, bf16[32,1,16,1024]{3,2,1,0:T(8,128)(2,1)} %all-to-all-done.2), kind=kOutput, calls=%fused_computation.4 | convolution fusion | flops 1610612736 | bytes 7340032 | tf_op jit(solution)/shard_map/sjcd,djf->sjcf/dot_general | solution.py:100
  169.0 1.6 all-to-all-done.1
  170.7 5.3 %fusion.29 = (bf16[32,16,768]{2,0,1:T(8,128)(2,1)S(1)}, bf16[32,16,768]{2,0,1:T(8,128)(2,1)S(1)}, bf16[32,1,16,768]{3,0,2,1:T(8,128)(2,1)}) fusion(f32[32,1,16,1536]{3,0,2,1:T(8,128)} %convolution_bitcast_fusion, bf16[32,1,16,1024]{3,2,1,0:T(8,128)(2,1)S(1)} %all-to-all-done.1, bf16[1,768,1024]{2,1,0:T(8,128)(2,1)S(1)} %copy-done.11, ...), kind=kOutput, calls=%fused_computation.46 | convolution fusion | flops 813957120 | bytes 8131584 | tf_op jit(solution)/shard_map/sjcd,jfd->sjcf/dot_general | solution.py:106
  176.0 3.8 fusion.15
  179.9 1.8 fusion.2
  181.6 3.0 copy.119
  184.7 1.4 copy-done.12
  186.0 2.2 fusion.12
  188.2 1.6 copy.109
  189.8 5.8 %all-to-all-start.4 = ((bf16[32,1,16,1024]{3,2,1,0:T(8,128)(2,1)}), bf16[32,1,16,1024]{3,2,1,0:T(8,128)(2,1)}, u32[]{:S(2)}, u32[]{:S(2)}) async-start(bf16[32,1,16,1024]{3,2,1,0:T(8,128)(2,1)} %copy.109), calls=%async_computation.4 | async-start | bytes 2097152 | tf_op jit(solution)/shard_map/all_to_all | solution.py:120
  195.9 4.1 fusion.11
  200.0 3.2 fusion.13
  203.2 1.6 copy.108
  204.7 7.1 %all-to-all-done.4 = bf16[32,1,16,1024]{3,2,1,0:T(8,128)(2,1)} async-done(((bf16[32,1,16,1024]{3,2,1,0:T(8,128)(2,1)}), bf16[32,1,16,1024]{3,2,1,0:T(8,128)(2,1)}, u32[]{:S(2)}, u32[]{:S(2)}) %all-to-all-start.4) | async-done | bytes 1048608 | tf_op jit(solution)/shard_map/all_to_all | solution.py:120
  211.8 5.0 %all-to-all-start.3 = ((bf16[32,1,16,1024]{3,2,1,0:T(8,128)(2,1)}), bf16[32,1,16,1024]{3,2,1,0:T(8,128)(2,1)S(1)}, u32[]{:S(2)}, u32[]{:S(2)}) async-start(bf16[32,1,16,1024]{3,2,1,0:T(8,128)(2,1)} %copy.108), calls=%async_computation.3 | async-start | bytes 2097152 | tf_op jit(solution)/shard_map/all_to_all | solution.py:115
  216.9 2.4 fusion.14
  219.3 13.8 %all-to-all-done.3 = bf16[32,1,16,1024]{3,2,1,0:T(8,128)(2,1)S(1)} async-done(((bf16[32,1,16,1024]{3,2,1,0:T(8,128)(2,1)}), bf16[32,1,16,1024]{3,2,1,0:T(8,128)(2,1)S(1)}, u32[]{:S(2)}, u32[]{:S(2)}) %all-to-all-start.3) | async-done | bytes 1048608 | tf_op jit(solution)/shard_map/all_to_all | solution.py:115
  233.1 1.0 convolution_convert_fusion.4
  234.1 23.1 %reduce-scatter.4.cloned.1.call-done = bf16[64,1536]{1,0:T(8,128)(2,1)} async-done(((bf16[1024,1536]{1,0:T(8,128)(2,1)}), bf16[64,1536]{1,0:T(8,128)(2,1)}) %reduce-scatter.4.cloned.1.call-update) | async-done | bytes 196624
  257.2 1.1 copy.120
  258.4 0.8 copy.111
  259.2 140.3 %all-reduce.2.cloned.1.call-done = bf16[1,768,1024]{2,1,0:T(8,128)(2,1)} async-done(((bf16[1,768,1024]{2,1,0:T(8,128)(2,1)}), bf16[1,768,1024]{2,1,0:T(8,128)(2,1)}) %all-reduce.2.cloned.1.call-update) | async-done | bytes 1572880 | tf_op jit(solution)/shard_map/psum | solution.py:136
  399.6 2.7 copy.147
  (63 shorter events, 4.2 us)
Async XLA Ops:
  7.2 67.7 %copy-start = (bf16[128,1024]{1,0:T(8,128)(2,1)S(1)}, bf16[128,1024]{1,0:T(8,128)(2,1)}, u32[]{:S(2)}) copy-start(bf16[128,1024]{1,0:T(8,128)(2,1)} %param.9) | copy-start | bytes 786436
  8.4 20.5 %collective-permute-start = (bf16[64,1,1536]{0,2,1:T(8,128)(2,1)S(1)}, bf16[64,1,1536]{0,2,1:T(8,128)(2,1)S(1)}, u32[]{:S(2)}, u32[]{:S(2)}) collective-permute-start(bf16[64,1,1536]{0,2,1:T(8,128)(2,1)S(1)} %copy.96), channel_id=1, source_target_pairs={{0,32},{32,64},{64,96},{96,128},{128,160},{160,192},{192,224},{224... | collective-permute-start | bytes 589832 | tf_op jit(solution)/shard_map/ppermute | solution.py:17
  12.2 27.8 %collective-permute-start.8 = (bf16[64,1,1536]{0,2,1:T(8,128)(2,1)S(1)}, bf16[64,1,1536]{0,2,1:T(8,128)(2,1)S(1)}, u32[]{:S(2)}, u32[]{:S(2)}) collective-permute-start(bf16[64,1,1536]{0,2,1:T(8,128)(2,1)S(1)} %copy.96), channel_id=1, source_target_pairs={{0,480},{32,0},{64,32},{96,64},{128,96},{160,128},{192,160},{224,1... | collective-permute-start | bytes 589832 | tf_op jit(solution)/shard_map/ppermute | solution.py:19
  24.6 22.6 %copy-start.8 = (s32[128,2]{0,1:T(2,128)}, s32[128,2]{0,1:T(2,128)S(1)}, u32[]{:S(2)}) copy-start(s32[128,2]{0,1:T(2,128)S(1)} %multiply_add_fusion) | copy-start | bytes 3076
  28.9 16.3 %collective-permute-start.1 = (bf16[64,1,1536]{0,2,1:T(8,128)(2,1)S(1)}, bf16[64,1,1536]{0,2,1:T(8,128)(2,1)S(1)}, u32[]{:S(2)}, u32[]{:S(2)}) collective-permute-start(bf16[64,1,1536]{0,2,1:T(8,128)(2,1)S(1)} %collective-permute-done), channel_id=1, source_target_pairs={{0,32},{32,64},{64,96},{96,128},{128,160},{160,192},{192,224},{224... | collective-permute-start | bytes 589832 | tf_op jit(solution)/shard_map/ppermute | solution.py:17
  32.4 43.9 %all-to-all-start = ((bf16[32,1,16]{2,1,0:T(2,128)(2,1)}), bf16[32,1,16]{2,1,0:T(2,128)(2,1)S(1)}, u32[]{:S(2)}, u32[]{:S(2)}) async-start(bf16[32,1,16]{2,1,0:T(2,128)(2,1)} %reshape.263), calls=%async_computation | async-start | bytes 32768 | tf_op jit(solution)/shard_map/all_to_all | solution.py:92
  40.1 13.8 %collective-permute-start.9 = (bf16[64,1,1536]{0,2,1:T(8,128)(2,1)S(1)}, bf16[64,1,1536]{0,2,1:T(8,128)(2,1)S(1)}, u32[]{:S(2)}, u32[]{:S(2)}) collective-permute-start(bf16[64,1,1536]{0,2,1:T(8,128)(2,1)S(1)} %collective-permute-done.8), channel_id=1, source_target_pairs={{0,480},{32,0},{64,32},{96,64},{128,96},{160,128},{192,160},{224,1... | collective-permute-start | bytes 589832 | tf_op jit(solution)/shard_map/ppermute | solution.py:19
  45.2 14.3 %collective-permute-start.2 = (bf16[64,1,1536]{0,2,1:T(8,128)(2,1)S(1)}, bf16[64,1,1536]{0,2,1:T(8,128)(2,1)S(1)}, u32[]{:S(2)}, u32[]{:S(2)}) collective-permute-start(bf16[64,1,1536]{0,2,1:T(8,128)(2,1)S(1)} %collective-permute-done.1), channel_id=1, source_target_pairs={{0,32},{32,64},{64,96},{96,128},{128,160},{160,192},{192,224},{224... | collective-permute-start | bytes 589832 | tf_op jit(solution)/shard_map/ppermute | solution.py:17
  53.9 13.4 %collective-permute-start.10 = (bf16[64,1,1536]{0,2,1:T(8,128)(2,1)S(1)}, bf16[64,1,1536]{0,2,1:T(8,128)(2,1)S(1)}, u32[]{:S(2)}, u32[]{:S(2)}) collective-permute-start(bf16[64,1,1536]{0,2,1:T(8,128)(2,1)S(1)} %collective-permute-done.9), channel_id=1, source_target_pairs={{0,480},{32,0},{64,32},{96,64},{128,96},{160,128},{192,160},{224,1... | collective-permute-start | bytes 589832 | tf_op jit(solution)/shard_map/ppermute | solution.py:19
  59.5 13.4 %collective-permute-start.3 = (bf16[64,1,1536]{0,2,1:T(8,128)(2,1)S(1)}, bf16[64,1,1536]{0,2,1:T(8,128)(2,1)S(1)}, u32[]{:S(2)}, u32[]{:S(2)}) collective-permute-start(bf16[64,1,1536]{0,2,1:T(8,128)(2,1)S(1)} %collective-permute-done.2), channel_id=1, source_target_pairs={{0,32},{32,64},{64,96},{96,128},{128,160},{160,192},{192,224},{224... | collective-permute-start | bytes 589832 | tf_op jit(solution)/shard_map/ppermute | solution.py:17
  67.3 17.3 %collective-permute-start.11 = (bf16[64,1,1536]{0,2,1:T(8,128)(2,1)S(1)}, bf16[64,1,1536]{0,2,1:T(8,128)(2,1)}, u32[]{:S(2)}, u32[]{:S(2)}) collective-permute-start(bf16[64,1,1536]{0,2,1:T(8,128)(2,1)S(1)} %collective-permute-done.10), channel_id=1, source_target_pairs={{0,480},{32,0},{64,32},{96,64},{128,96},{160,128},{192,160},{224,1... | collective-permute-start | bytes 589832 | tf_op jit(solution)/shard_map/ppermute | solution.py:19
  72.9 16.8 %collective-permute-start.4 = (bf16[64,1,1536]{0,2,1:T(8,128)(2,1)S(1)}, bf16[64,1,1536]{0,2,1:T(8,128)(2,1)}, u32[]{:S(2)}, u32[]{:S(2)}) collective-permute-start(bf16[64,1,1536]{0,2,1:T(8,128)(2,1)S(1)} %collective-permute-done.3), channel_id=1, source_target_pairs={{0,32},{32,64},{64,96},{96,128},{128,160},{160,192},{192,224},{224... | collective-permute-start | bytes 589832 | tf_op jit(solution)/shard_map/ppermute | solution.py:17
  76.3 70.9 %all-to-all-start.2 = ((bf16[32,1,16,1024]{3,2,1,0:T(8,128)(2,1)}), bf16[32,1,16,1024]{3,2,1,0:T(8,128)(2,1)}, u32[]{:S(2)}, u32[]{:S(2)}) async-start(bf16[32,1,16,1024]{3,2,1,0:T(8,128)(2,1)} %bitcast.20), calls=%async_computation.2 | async-start | bytes 2097152 | tf_op jit(solution)/shard_map/all_to_all | solution.py:90
  84.6 14.1 %collective-permute-start.12 = (bf16[64,1,1536]{0,2,1:T(8,128)(2,1)}, bf16[64,1,1536]{0,2,1:T(8,128)(2,1)}, u32[]{:S(2)}, u32[]{:S(2)}) collective-permute-start(bf16[64,1,1536]{0,2,1:T(8,128)(2,1)} %collective-permute-done.11), channel_id=1, source_target_pairs={{0,480},{32,0},{64,32},{96,64},{128,96},{160,128},{192,160},{224,1... | collective-permute-start | bytes 589832 | tf_op jit(solution)/shard_map/ppermute | solution.py:19
  89.7 14.6 %collective-permute-start.5 = (bf16[64,1,1536]{0,2,1:T(8,128)(2,1)}, bf16[64,1,1536]{0,2,1:T(8,128)(2,1)}, u32[]{:S(2)}, u32[]{:S(2)}) collective-permute-start(bf16[64,1,1536]{0,2,1:T(8,128)(2,1)} %collective-permute-done.4), channel_id=1, source_target_pairs={{0,32},{32,64},{64,96},{96,128},{128,160},{160,192},{192,224},{224... | collective-permute-start | bytes 589832 | tf_op jit(solution)/shard_map/ppermute | solution.py:17
  98.7 13.7 %collective-permute-start.13 = (bf16[64,1,1536]{0,2,1:T(8,128)(2,1)}, bf16[64,1,1536]{0,2,1:T(8,128)(2,1)}, u32[]{:S(2)}, u32[]{:S(2)}) collective-permute-start(bf16[64,1,1536]{0,2,1:T(8,128)(2,1)} %collective-permute-done.12), channel_id=1, source_target_pairs={{0,480},{32,0},{64,32},{96,64},{128,96},{160,128},{192,160},{224,1... | collective-permute-start | bytes 589832 | tf_op jit(solution)/shard_map/ppermute | solution.py:19
  104.3 13.7 %collective-permute-start.6 = (bf16[64,1,1536]{0,2,1:T(8,128)(2,1)}, bf16[64,1,1536]{0,2,1:T(8,128)(2,1)}, u32[]{:S(2)}, u32[]{:S(2)}) collective-permute-start(bf16[64,1,1536]{0,2,1:T(8,128)(2,1)} %collective-permute-done.5), channel_id=1, source_target_pairs={{0,32},{32,64},{64,96},{96,128},{128,160},{160,192},{192,224},{224... | collective-permute-start | bytes 589832 | tf_op jit(solution)/shard_map/ppermute | solution.py:17
  112.4 12.8 %collective-permute-start.14 = (bf16[64,1,1536]{0,2,1:T(8,128)(2,1)}, bf16[64,1,1536]{0,2,1:T(8,128)(2,1)}, u32[]{:S(2)}, u32[]{:S(2)}) collective-permute-start(bf16[64,1,1536]{0,2,1:T(8,128)(2,1)} %collective-permute-done.13), channel_id=1, source_target_pairs={{0,480},{32,0},{64,32},{96,64},{128,96},{160,128},{192,160},{224,1... | collective-permute-start | bytes 589832 | tf_op jit(solution)/shard_map/ppermute | solution.py:19
  118.1 12.6 %collective-permute-start.7 = (bf16[64,1,1536]{0,2,1:T(8,128)(2,1)}, bf16[64,1,1536]{0,2,1:T(8,128)(2,1)}, u32[]{:S(2)}, u32[]{:S(2)}) collective-permute-start(bf16[64,1,1536]{0,2,1:T(8,128)(2,1)} %collective-permute-done.6), channel_id=1, source_target_pairs={{0,32},{32,64},{64,96},{96,128},{128,160},{160,192},{192,224},{224... | collective-permute-start | bytes 589832 | tf_op jit(solution)/shard_map/ppermute | solution.py:17
  147.1 7.7 %copy-start.7 = (f32[1,2,8,128]{3,1,2,0:T(2,128)S(1)}, f32[1,2,8,128]{3,1,2,0:T(2,128)}, u32[]{:S(2)}) copy-start(f32[1,2,8,128]{3,1,2,0:T(2,128)} %copy.145) | copy-start | bytes 24580
  147.2 23.5 %all-to-all-start.1 = ((bf16[32,1,16,1024]{3,2,1,0:T(8,128)(2,1)}), bf16[32,1,16,1024]{3,2,1,0:T(8,128)(2,1)S(1)}, u32[]{:S(2)}, u32[]{:S(2)}) async-start(bf16[32,1,16,1024]{3,2,1,0:T(8,128)(2,1)} %bitcast.14), calls=%async_computation.1 | async-start | bytes 2097152 | tf_op jit(solution)/shard_map/all_to_all | solution.py:91
  154.6 102.7 %reduce-scatter.4.cloned.1.call-start = ((), (), s32[]{:S(2)}) async-start(), calls=%async_computation.7 | async-start | bytes 3342336
  154.8 5.1 %copy-start.2 = (bf16[2048,1,1536]{0,2,1:T(8,128)(2,1)S(1)}, bf16[2048,1,1536]{0,2,1:T(8,128)(2,1)}, u32[]{:S(2)}) copy-start(bf16[2048,1,1536]{0,2,1:T(8,128)(2,1)} %concatenate.18) | copy-start | bytes 18874372
  155.6 6.4 %copy-start.1 = (f32[1024,2,768]{0,2,1:T(8,128)}, f32[1024,2,768]{0,2,1:T(8,128)S(1)}, u32[]{:S(2)}) copy-start(f32[1024,2,768]{0,2,1:T(8,128)S(1)} %broadcast_in_dim.28) | copy-start | bytes 18874372
  162.0 1.7 copy-start.3
  163.7 6.9 %copy-start.10 = (f32[768]{0:T(1024)S(1)}, f32[768]{0:T(1024)}, u32[]{:S(2)}) copy-start(f32[768]{0:T(1024)} %broadcast_bitcast_fusion.1) | copy-start | bytes 9220
  163.7 6.9 %copy-start.11 = (bf16[1,768,1024]{2,1,0:T(8,128)(2,1)S(1)}, bf16[1,768,1024]{2,1,0:T(8,128)(2,1)}, u32[]{:S(2)}) copy-start(bf16[1,768,1024]{2,1,0:T(8,128)(2,1)} %param.14) | copy-start | bytes 4718596
  170.7 5.3 %copy-start.5 = (bf16[32,1,16,1024]{3,2,1,0:T(8,128)(2,1)}, bf16[32,1,16,1024]{3,2,1,0:T(8,128)(2,1)S(1)}, u32[]{:S(2)}) copy-start(bf16[32,1,16,1024]{3,2,1,0:T(8,128)(2,1)S(1)} %all-to-all-done.1) | copy-start | bytes 3145732
  170.7 9.2 %slice-start = ((s8[6291456]{0:T(1024)(128)(4,1)}), s8[4194304]{0:T(1024)(128)(4,1)S(1)}, s32[]{:S(2)}) async-start(s8[6291456]{0:T(1024)(128)(4,1)} %bitcast.155), calls=%async_computation.8 | async-start | bytes 8388608
  176.0 3.9 copy-start.13
  176.0 3.9 copy-start.14
  176.0 3.9 slice-start.1
  184.6 1.4 copy-start.12
  189.8 22.0 %all-to-all-start.4 = ((bf16[32,1,16,1024]{3,2,1,0:T(8,128)(2,1)}), bf16[32,1,16,1024]{3,2,1,0:T(8,128)(2,1)}, u32[]{:S(2)}, u32[]{:S(2)}) async-start(bf16[32,1,16,1024]{3,2,1,0:T(8,128)(2,1)} %copy.109), calls=%async_computation.4 | async-start | bytes 2097152 | tf_op jit(solution)/shard_map/all_to_all | solution.py:120
  195.6 4.4 %copy-start.4 = (bf16[1024,1536,1]{0,1,2:T(8,128)(2,1)S(1)}, bf16[1024,1536,1]{0,1,2:T(8,128)(2,1)}, u32[]{:S(2)}) copy-start(bf16[1024,1536,1]{0,1,2:T(8,128)(2,1)} %copy-done.3) | copy-start | bytes 9437188
  195.6 203.9 %all-reduce.2.cloned.1.call-start = ((), (), s32[]{:S(2)}) async-start(), calls=%async_computation.6 | async-start | bytes 3145728 | tf_op jit(solution)/shard_map/psum | solution.py:136
  203.2 13.7 %copy-start.6 = (bf16[128,1024]{1,0:T(8,128)(2,1)S(1)}, bf16[128,1024]{1,0:T(8,128)(2,1)}, u32[]{:S(2)}) copy-start(bf16[128,1024]{1,0:T(8,128)(2,1)} %param.10) | copy-start | bytes 786436
  203.2 13.8 %copy-start.9 = (s32[128,2]{0,1:T(2,128)S(1)}, s32[128,2]{0,1:T(2,128)}, u32[]{:S(2)}) copy-start(s32[128,2]{0,1:T(2,128)} %copy-done.8) | copy-start | bytes 3076
  211.8 21.3 %all-to-all-start.3 = ((bf16[32,1,16,1024]{3,2,1,0:T(8,128)(2,1)}), bf16[32,1,16,1024]{3,2,1,0:T(8,128)(2,1)S(1)}, u32[]{:S(2)}, u32[]{:S(2)}) async-start(bf16[32,1,16,1024]{3,2,1,0:T(8,128)(2,1)} %copy.108), calls=%async_computation.3 | async-start | bytes 2097152 | tf_op jit(solution)/shard_map/all_to_all | solution.py:115
Sparse Core Ops, SparseCore 0:
  184.8 72.4 reduce-scatter.3
  260.2 139.3 all-reduce.1
